TPU v7x, 32 devices: a whole 2x2x4 slice. The times are simulated.
32 devices in a mesh: dp: 16 (over z, y, x), tensor: 2 (over core).
Axes of the slice: x: 2, y: 2, z: 4, core: 2. Of those that a mesh axis runs over, the one named last changes fastest.
Arguments:
- tokens: bfloat16 [16384, 768], P(('dp', 'tensor')), may hold values from -6 to 6
- lengths: int32 [48], replicated, may hold values from 32 to 1024, as said below
- owners: int32 [48], replicated, may hold values from 0 to 15
- gain_first: bfloat16 [768], replicated, may hold values from 0.5 to 1.5
- shift_first: bfloat16 [768], replicated, may hold values from -1.1953125 to 1.1953125
- query_weight: bfloat16 [768, 768], P(None, 'tensor'), may hold values from -0.21875 to 0.21875
- key_weight: bfloat16 [768, 768], P(None, 'tensor'), may hold values from -0.21875 to 0.21875
- value_weight: bfloat16 [768, 768], P(None, 'tensor'), may hold values from -0.21875 to 0.21875
- query_bias: bfloat16 [768], P('tensor'), may hold values from -1.1953125 to 1.1953125
- value_bias: bfloat16 [768], P('tensor'), may hold values from -1.1953125 to 1.1953125
- output_weight: bfloat16 [768, 768], P('tensor'), may hold values from -2.5 to 2.5
- output_bias: bfloat16 [768], replicated, may hold values from -1.1953125 to 1.1953125
- gain_second: bfloat16 [768], replicated, may hold values from 0.5 to 1.5
- shift_second: bfloat16 [768], replicated, may hold values from -1.1953125 to 1.1953125
- expand_weight: bfloat16 [768, 3072], P(None, 'tensor'), may hold values from -0.21875 to 0.21875
- expand_bias: bfloat16 [3072], P('tensor'), may hold values from -1.1953125 to 1.1953125
- contract_weight: bfloat16 [3072, 768], P('tensor'), may hold values from -0.15625 to 0.15625
- contract_bias: bfloat16 [768], replicated, may hold values from -1.1953125 to 1.1953125
- cotangent: bfloat16 [16384, 768], P(('dp', 'tensor')), may hold values from -6 to 6
Outputs:
- result: bfloat16 [16384, 768], P(('dp', 'tensor'))
- tokens_grad: bfloat16 [16384, 768], P(('dp', 'tensor'))
- gain_first_grad: float32 [768], replicated
- shift_first_grad: float32 [768], replicated
- query_weight_grad: float32 [768, 768], P(None, 'tensor')
- key_weight_grad: float32 [768, 768], P(None, 'tensor')
- value_weight_grad: float32 [768, 768], P(None, 'tensor')
- query_bias_grad: float32 [768], P('tensor')
- value_bias_grad: float32 [768], P('tensor')
- output_weight_grad: float32 [768, 768], P('tensor')
- output_bias_grad: float32 [768], replicated
- gain_second_grad: float32 [768], replicated
- shift_second_grad: float32 [768], replicated
- expand_weight_grad: float32 [768, 3072], P(None, 'tensor')
- expand_bias_grad: float32 [3072], P('tensor')
- contract_weight_grad: float32 [3072, 768], P('tensor')
- contract_bias_grad: float32 [768], replicated
Inputs may be any that keep to these rules, and one draw needn't show every extreme that they name: Sequence i has lengths[i] tokens and lies in data group owners[i]; the sequences of a group follow one another in order of their index from the group's first row, and rows after them belong to no sequence. The lengths of a group sum to at most 1024; every group holds at least one sequence; in every draw one group holds a single sequence of exactly 1024 tokens.
All inputs are finite; a program needn't handle non-finite values.
Results may differ from a plain program's by a relative error of at most 0.012.
Values may be sent and summed in bfloat16 or wider, within the bound.
A program may use at most 128 MiB of HBM per device.

v0:
```python
import jax
import jax.numpy as jnp
from jax import lax
from jax.sharding import PartitionSpec as P

HD = 64
CAP = 1024


epsilon = 1e-05


def layer_norm(values, gain, shift):
    average = jnp.mean(values, axis=-1, keepdims=True)
    centred = values - average
    variance = jnp.mean(centred * centred, axis=-1, keepdims=True)
    return centred * lax.rsqrt(variance + epsilon) * gain + shift


def gelu_tanh(values):
    return jax.nn.gelu(values, approximate=True)


def row_segments(lengths, owners, group, total_rows):
    count = lengths.shape[0]
    index = jnp.arange(count, dtype=jnp.int32)
    same = owners[None, :] == owners[:, None]
    earlier = index[None, :] < index[:, None]
    starts = jnp.sum(jnp.where(same & earlier, lengths[None, :], 0), axis=1, dtype=jnp.int32)
    positions = jnp.arange(total_rows, dtype=jnp.int32)[:, None]
    inside = (
        (owners[None, :] == group)
        & (positions >= starts[None, :])
        & (positions < starts[None, :] + lengths[None, :])
    )
    return jnp.sum(jnp.where(inside, index[None, :] + 1, 0), axis=1, dtype=jnp.int32)


def rows_product(left, right):
    return lax.dot_general(
        left, right, (((0,), (0,)), ((), ())), preferred_element_type=jnp.float32
    )


def transposed_product(left, right):
    return lax.dot_general(
        left, right, (((1,), (1,)), ((), ())), preferred_element_type=jnp.float32
    )


def masked_scores(query_block, keys, segment_block, segments, start, scale):
    block = query_block.shape[0]
    positions = jnp.arange(keys.shape[0], dtype=jnp.int32)
    rows_here = start + jnp.arange(block, dtype=jnp.int32)
    allowed = (segment_block[:, None] == segments[None, :]) & (
        positions[None, :] <= rows_here[:, None]
    )
    scaled = (
        jnp.einsum("qhd,khd->hqk", query_block, keys, preferred_element_type=jnp.float32) * scale
    )
    return jnp.where(allowed[None], scaled, -1e30)


def attention_forward(query, keys, values, segments, scale):
    total_rows = query.shape[0]
    block = min(512, total_rows)
    count = total_rows // block

    def one(index):
        start = index * block
        query_block = lax.dynamic_slice_in_dim(query, start, block, 0)
        segment_block = lax.dynamic_slice_in_dim(segments, start, block, 0)
        scores = masked_scores(query_block, keys, segment_block, segments, start, scale)
        top = jnp.max(scores, axis=-1, keepdims=True)
        powers = jnp.exp(scores - top)
        totals = jnp.sum(powers, axis=-1, keepdims=True)
        probs = (powers / totals).astype(jnp.bfloat16)
        mixed = jnp.einsum("hqk,khd->qhd", probs, values, preferred_element_type=jnp.float32)
        return (mixed, top[..., 0], totals[..., 0])

    mixed, tops, totals = lax.map(one, jnp.arange(count, dtype=jnp.int32))
    return (mixed.reshape(total_rows, -1), tops, totals)


def attention_backward(query, keys, values, segments, tops, totals, grad_mixed, scale):
    total_rows, heads, size = query.shape
    block = min(512, total_rows)
    count = total_rows // block

    def one(carry, index):
        key_sum, value_sum = carry
        start = index * block
        query_block = lax.dynamic_slice_in_dim(query, start, block, 0)
        segment_block = lax.dynamic_slice_in_dim(segments, start, block, 0)
        grad_block = lax.dynamic_slice_in_dim(grad_mixed, start, block, 0)
        scores = masked_scores(query_block, keys, segment_block, segments, start, scale)
        probs = jnp.exp(scores - tops[index][..., None]) / totals[index][..., None]
        grad_probs = jnp.einsum(
            "qhd,khd->hqk", grad_block, values, preferred_element_type=jnp.float32
        )
        inner = jnp.sum(probs * grad_probs, axis=-1, keepdims=True)
        grad_scores = (probs * (grad_probs - inner)).astype(jnp.bfloat16)
        query_part = (
            jnp.einsum("hqk,khd->qhd", grad_scores, keys, preferred_element_type=jnp.float32)
            * scale
        )
        key_sum = (
            key_sum
            + jnp.einsum(
                "hqk,qhd->khd", grad_scores, query_block, preferred_element_type=jnp.float32
            )
            * scale
        )
        value_sum = value_sum + jnp.einsum(
            "hqk,qhd->khd",
            probs.astype(jnp.bfloat16),
            grad_block,
            preferred_element_type=jnp.float32,
        )
        return ((key_sum, value_sum), query_part)

    empty = jnp.zeros((total_rows, heads, size), jnp.float32)
    (key_sum, value_sum), query_parts = lax.scan(
        one, (empty, empty), jnp.arange(count, dtype=jnp.int32)
    )
    width = heads * size
    return (
        query_parts.reshape(total_rows, width).astype(jnp.bfloat16),
        key_sum.reshape(total_rows, width).astype(jnp.bfloat16),
        value_sum.reshape(total_rows, width).astype(jnp.bfloat16),
    )


def on_device(
    tokens,
    lengths,
    owners,
    gain_first,
    shift_first,
    query_weight,
    key_weight,
    value_weight,
    query_bias,
    value_bias,
    output_weight,
    output_bias,
    gain_second,
    shift_second,
    expand_weight,
    expand_bias,
    contract_weight,
    contract_bias,
    cotangent,
):
    own_rows = tokens.shape[0]
    group = lax.axis_index("dp")
    first_row = lax.axis_index("tensor") * own_rows
    segments = row_segments(lengths, owners, group, CAP)
    own_segments = lax.dynamic_slice_in_dim(segments, first_row, own_rows, 0)
    live = (own_segments > 0).astype(jnp.float32)[:, None]
    heads = query_weight.shape[1] // HD
    scale = HD ** (-0.5)
    split = (CAP, heads, HD)
    inputs = tokens.astype(jnp.float32)
    normed_value, pull_first = jax.vjp(
        layer_norm, inputs, gain_first.astype(jnp.float32), shift_first.astype(jnp.float32)
    )
    normed = lax.all_gather(normed_value.astype(jnp.bfloat16), "tensor", axis=0, tiled=True)
    query = (
        jnp.dot(normed, query_weight, preferred_element_type=jnp.float32)
        + query_bias.astype(jnp.float32)
    ).astype(jnp.bfloat16)
    keys = jnp.dot(normed, key_weight, preferred_element_type=jnp.float32).astype(jnp.bfloat16)
    values = (
        jnp.dot(normed, value_weight, preferred_element_type=jnp.float32)
        + value_bias.astype(jnp.float32)
    ).astype(jnp.bfloat16)
    mixed, tops, totals = attention_forward(
        query.reshape(split), keys.reshape(split), values.reshape(split), segments, scale
    )
    mixed = mixed.astype(jnp.bfloat16)
    branch = lax.psum_scatter(
        jnp.dot(mixed, output_weight, preferred_element_type=jnp.float32),
        "tensor",
        scatter_dimension=0,
        tiled=True,
    ) + output_bias.astype(jnp.float32)
    hidden = inputs + live * branch
    middle_value, pull_second = jax.vjp(
        layer_norm, hidden, gain_second.astype(jnp.float32), shift_second.astype(jnp.float32)
    )
    middle = lax.all_gather(middle_value.astype(jnp.bfloat16), "tensor", axis=0, tiled=True)
    before = jnp.dot(
        middle, expand_weight, preferred_element_type=jnp.float32
    ) + expand_bias.astype(jnp.float32)
    active_value, pull_active = jax.vjp(gelu_tanh, before)
    active = active_value.astype(jnp.bfloat16)
    branch_two = lax.psum_scatter(
        jnp.dot(active, contract_weight, preferred_element_type=jnp.float32).astype(jnp.bfloat16),
        "tensor",
        scatter_dimension=0,
        tiled=True,
    ).astype(jnp.float32) + contract_bias.astype(jnp.float32)
    result = (hidden + live * branch_two).astype(jnp.bfloat16)
    upstream = cotangent.astype(jnp.float32)
    grad_two = lax.all_gather((live * upstream).astype(jnp.bfloat16), "tensor", axis=0, tiled=True)
    contract_weight_grad = rows_product(active, grad_two)
    contract_bias_grad = jnp.sum(grad_two, axis=0, dtype=jnp.float32)
    grad_before = pull_active(transposed_product(grad_two, contract_weight))[0].astype(jnp.bfloat16)
    expand_weight_grad = rows_product(middle, grad_before)
    expand_bias_grad = jnp.sum(grad_before, axis=0, dtype=jnp.float32)
    grad_middle = lax.psum_scatter(
        transposed_product(grad_before, expand_weight), "tensor", scatter_dimension=0, tiled=True
    )
    grad_norm_two, gain_second_grad, shift_second_grad = pull_second(grad_middle)
    grad_hidden = upstream + grad_norm_two
    grad_branch = lax.all_gather(
        (live * grad_hidden).astype(jnp.bfloat16), "tensor", axis=0, tiled=True
    )
    output_weight_grad = rows_product(mixed, grad_branch)
    output_bias_grad = jnp.sum(grad_branch, axis=0, dtype=jnp.float32)
    grad_mixed = transposed_product(grad_branch, output_weight).astype(jnp.bfloat16)
    grad_query, grad_keys, grad_values = attention_backward(
        query.reshape(split),
        keys.reshape(split),
        values.reshape(split),
        segments,
        tops,
        totals,
        grad_mixed.reshape(split),
        scale,
    )
    query_weight_grad = rows_product(normed, grad_query)
    key_weight_grad = rows_product(normed, grad_keys)
    value_weight_grad = rows_product(normed, grad_values)
    query_bias_grad = jnp.sum(grad_query, axis=0, dtype=jnp.float32)
    value_bias_grad = jnp.sum(grad_values, axis=0, dtype=jnp.float32)
    grad_normed = lax.psum_scatter(
        transposed_product(grad_query, query_weight)
        + transposed_product(grad_keys, key_weight)
        + transposed_product(grad_values, value_weight),
        "tensor",
        scatter_dimension=0,
        tiled=True,
    )
    grad_norm_one, gain_first_grad, shift_first_grad = pull_first(grad_normed)
    tokens_grad = (grad_hidden + grad_norm_one).astype(jnp.bfloat16)
    gain_first_grad, shift_first_grad, gain_second_grad, shift_second_grad = lax.psum(
        (gain_first_grad, shift_first_grad, gain_second_grad, shift_second_grad), ("dp", "tensor")
    )
    (
        expand_weight_grad,
        expand_bias_grad,
        contract_weight_grad,
        contract_bias_grad,
        query_weight_grad,
        key_weight_grad,
        value_weight_grad,
        query_bias_grad,
        value_bias_grad,
        output_weight_grad,
        output_bias_grad,
    ) = lax.psum(
        (
            expand_weight_grad,
            expand_bias_grad,
            contract_weight_grad,
            contract_bias_grad,
            query_weight_grad,
            key_weight_grad,
            value_weight_grad,
            query_bias_grad,
            value_bias_grad,
            output_weight_grad,
            output_bias_grad,
        ),
        "dp",
    )
    return (
        result,
        tokens_grad,
        gain_first_grad,
        shift_first_grad,
        query_weight_grad,
        key_weight_grad,
        value_weight_grad,
        query_bias_grad,
        value_bias_grad,
        output_weight_grad,
        output_bias_grad,
        gain_second_grad,
        shift_second_grad,
        expand_weight_grad,
        expand_bias_grad,
        contract_weight_grad,
        contract_bias_grad,
    )


def solution(mesh):
    in_specs = (
        P(("dp", "tensor"), None),
        P(),
        P(),
        P(),
        P(),
        P(None, "tensor"),
        P(None, "tensor"),
        P(None, "tensor"),
        P("tensor"),
        P("tensor"),
        P("tensor", None),
        P(),
        P(),
        P(),
        P(None, "tensor"),
        P("tensor"),
        P("tensor", None),
        P(),
        P(("dp", "tensor"), None),
    )
    out_specs = (
        P(("dp", "tensor"), None),
        P(("dp", "tensor"), None),
        P(),
        P(),
        P(None, "tensor"),
        P(None, "tensor"),
        P(None, "tensor"),
        P("tensor"),
        P("tensor"),
        P("tensor", None),
        P(),
        P(),
        P(),
        P(None, "tensor"),
        P("tensor"),
        P("tensor", None),
        P(),
    )
    return jax.shard_map(
        on_device, mesh=mesh, in_specs=in_specs, out_specs=out_specs, check_vma=False
    )
```

profile of v0, /device:TPU:0, one launch (start us, length us, event | category | flops | bytes accessed | tf_op | source)
XLA Modules:
  0.0 683.8 jit_solution(13047537237785481250)
XLA Ops:
  13.3 12.2 %all-gather.5.cloned.1.call-done = bf16[1024,768]{1,0:T(8,128)(2,1)} async-done(((bf16[512,768]{1,0:T(8,128)(2,1)}), bf16[1024,768]{1,0:T(8,128)(2,1)}) %all-gather.5.cloned.1.call-update) | async-done | bytes 1572880 | tf_op jit(solution)/shard_map/all_gather | solution.py:168
  32.4 28.6 %while.29 = (s32[]{:T(128)}, bf16[2,512,6,64]{1,3,2,0:T(8,128)(2,1)}, f32[2,6,512]{2,1,0:T(8,128)S(1)}, f32[2,6,512]{2,1,0:T(8,128)S(1)}, s32[2]{0:T(128)S(1)}, ...) while((s32[]{:T(128)}, ...), condition=%wide.region_7.8_spmd, body=%wide.region_4.7_spmd.sunk | while | flops 844622336 | bytes 52185380 | solution.py:81
  41.4 4.4 fusion.134
  55.7 4.4 fusion.134
  67.5 11.5 %reduce-scatter.5.cloned.1.call-done = f32[512,768]{1,0:T(8,128)} async-done(((f32[1024,768]{1,0:T(8,128)}), f32[512,768]{1,0:T(8,128)}) %reduce-scatter.5.cloned.1.call-update) | async-done | bytes 1572880 | tf_op jit(solution)/shard_map/reduce_scatter | solution.py:182
  85.2 10.5 %all-gather.7.cloned.1.call-done = bf16[1024,768]{1,0:T(8,128)(2,1)} async-done(((bf16[512,768]{1,0:T(8,128)(2,1)}), bf16[1024,768]{1,0:T(8,128)(2,1)}) %all-gather.7.cloned.1.call-update) | async-done | bytes 1572880 | tf_op jit(solution)/shard_map/all_gather | solution.py:192
  95.6 7.4 %fusion.58 = f32[1024,1536]{1,0:T(8,128)} fusion(bf16[1024,768]{1,0:T(8,128)(2,1)} %all-gather.7.cloned.1.call-done, bf16[768,1536]{1,0:T(8,128)(2,1)} %param.37), kind=kOutput, calls=%fused_computation.116 | convolution fusion | flops 2415919104 | bytes 10223616 | tf_op jit(solution)/shard_map/dot_general | solution.py:193
  103.0 5.7 all-gather.9.cloned.1.call-done
  108.7 10.6 %convert_reduce_fusion = (f32[1536]{0:T(1024)}, bf16[1024,1536]{1,0:T(8,128)(2,1)S(1)}, bf16[1024,1536]{1,0:T(8,128)(2,1)}) fusion(f32[1024,1536]{1,0:T(8,128)} %fusion.58, f32[1536]{0:T(1024)S(1)} %convert_element_type.146, bf16[1024,768]{1,0:T(8,128)(2,1)} %all-gather.9.cloned.1.call-done, bf16[1536,768]{1,0:T(8,128)(2,1)S(1)} %copy-done), kind=kOutput, calls=%fused_computation.51 | convolution fusion | flops 2455239168 | bytes 16527360 | tf_op jit(solution)/shard_map/dot_general | solution.py:46
  125.4 5.7 convolution_convert_fusion
  131.8 5.8 reduce-scatter.9.cloned.1.call-done
  140.2 9.7 %reduce-scatter.7.cloned.1.call-done = bf16[512,768]{1,0:T(8,128)(2,1)} async-done(((bf16[1024,768]{1,0:T(8,128)(2,1)}), bf16[512,768]{1,0:T(8,128)(2,1)}) %reduce-scatter.7.cloned.1.call-update) | async-done | bytes 786448 | tf_op jit(solution)/shard_map/reduce_scatter | solution.py:198
  155.8 11.1 %all-gather.11.cloned.1.call-done = bf16[1024,768]{1,0:T(8,128)(2,1)} async-done(((bf16[512,768]{1,0:T(8,128)(2,1)}), bf16[1024,768]{1,0:T(8,128)(2,1)}) %all-gather.11.cloned.1.call-update) | async-done | bytes 1572880 | tf_op jit(solution)/shard_map/all_gather | solution.py:217
  171.0 61.6 %while.30 = (s32[]{:T(128)}, f32[1024,6,64]{0,2,1:T(8,128)S(1)}, f32[1024,6,64]{0,2,1:T(8,128)}, bf16[2,512,6,64]{1,3,2,0:T(8,128)(2,1)}, s32[2]{0:T(128)S(1)}, ...) while((s32[]{:T(128)}, f32[1024,6,64]{0,2,1:T(8,128)S(1)}, ...), condition=%wide.region_17.18_spmd.clone, body=%wide.region_15.17_spmd.clone.sunk | while | flops 2048456192 | bytes 128571832 | solution.py:123
  175.1 7.6 %fusion.144 = f32[6,512,1024]{2,1,0:T(8,128)} fusion(bf16[1024,6,64]{0,2,1:T(8,128)(2,1)} %get-tuple-element.486, bf16[1024,6,64]{0,2,1:T(8,128)(2,1)} %get-tuple-element.485, s32[]{:T(128)S(6)} %select_n.64), kind=kOutput, calls=%fused_computation.31.clone.1 | convolution fusion | flops 402653184 | bytes 13762564 | tf_op jit(solution)/shard_map/while/body/eval_jaxpr/qhd,khd->hqk/dot_general | solution.py:98
  182.7 8.2 %multiply_reduce_fusion.5 = (f32[6,512]{1,0:T(8,128)S(1)}, f32[6,512,1024]{2,1,0:T(8,128)S(1)}) fusion(f32[6,512,1024]{2,1,0:T(8,128)} %fusion.144, f32[6,512]{1,0:T(8,128)S(1)} %get-tuple-element.398, f32[6,512]{1,0:T(8,128)S(1)} %get-tuple-element.399, bf16[1024,6,64]{0,2,1:T(8,128)(2,1)S(1)} %get-tuple-element.482, ...), kind=kOutput, calls=%fused_computation.19.clone.1 | convolution fusion | flops 421524480 | bytes 26914820 | tf_op jit(solution)/shard_map/while/body/eval_jaxpr/qhd,khd->hqk/dot_general | solution.py:59
  191.0 6.0 multiply_convert_fusion.4
  205.8 7.6 %fusion.144 = f32[6,512,1024]{2,1,0:T(8,128)} fusion(bf16[1024,6,64]{0,2,1:T(8,128)(2,1)} %get-tuple-element.486, bf16[1024,6,64]{0,2,1:T(8,128)(2,1)} %get-tuple-element.485, s32[]{:T(128)S(6)} %select_n.64), kind=kOutput, calls=%fused_computation.31.clone.1 | convolution fusion | flops 402653184 | bytes 13762564 | tf_op jit(solution)/shard_map/while/body/eval_jaxpr/qhd,khd->hqk/dot_general | solution.py:98
  213.4 8.3 %multiply_reduce_fusion.5 = (f32[6,512]{1,0:T(8,128)S(1)}, f32[6,512,1024]{2,1,0:T(8,128)S(1)}) fusion(f32[6,512,1024]{2,1,0:T(8,128)} %fusion.144, f32[6,512]{1,0:T(8,128)S(1)} %get-tuple-element.398, f32[6,512]{1,0:T(8,128)S(1)} %get-tuple-element.399, bf16[1024,6,64]{0,2,1:T(8,128)(2,1)S(1)} %get-tuple-element.482, ...), kind=kOutput, calls=%fused_computation.19.clone.1 | convolution fusion | flops 421524480 | bytes 26914820 | tf_op jit(solution)/shard_map/while/body/eval_jaxpr/qhd,khd->hqk/dot_general | solution.py:59
  221.7 6.0 multiply_convert_fusion.4
  241.7 7.6 %fusion.67 = f32[1536,768]{1,0:T(8,128)} fusion(bf16[1024,1536]{1,0:T(8,128)(2,1)} %get-tuple-element.255, bf16[1024,768]{1,0:T(8,128)(2,1)} %all-gather.9.cloned.1.call-done), kind=kOutput, calls=%fused_computation.125 | convolution fusion | flops 2415919104 | bytes 9437184 | tf_op jit(solution)/shard_map/dot_general | solution.py:40
  266.2 81.7 %all-reduce.1 = (f32[384]{0:T(512)}, f32[384]{0:T(512)}, f32[768]{0:T(1024)}, f32[1536]{0:T(1024)}, f32[768]{0:T(1024)}) all-reduce(f32[384]{0:T(512)S(1)} %reduce_sum.238, f32[384]{0:T(512)S(1)} %reduce_sum.240, f32[768]{0:T(1024)S(1)} %convert_reduce_fusion.2, ...), channel_id=1, replica_groups=mesh['dp'=16,'tensor'=2] {'dp'}, use_global_device_ids=true, to_apply=%region_29.30 | all-reduce | flops 3840 | bytes 30720 | tf_op jit(solution)/shard_map/psum | solution.py:263
  351.0 40.6 %all-reduce = (f32[768]{0:T(1024)}, f32[768]{0:T(1024)}, f32[768]{0:T(1024)}, f32[768]{0:T(1024)}) all-reduce(f32[768]{0:T(1024)S(1)} %get-tuple-element.177, f32[768]{0:T(1024)S(1)} %get-tuple-element.180, f32[768]{0:T(1024)S(1)} %copy-done.55, f32[768]{0:T(1024)S(1)} %copy-done.56), channel_id=1, replica_groups=mesh['dp'=16,'tensor'=2] {'dp','tensor'}, use_global_device_ids=true, to_apply=%region_22.23 | all-reduce | flops 3072 | bytes 24576 | tf_op jit(solution)/shard_map/psum | solution.py:248
  394.6 270.2 %all-reduce.5.cloned.1.call-done = (f32[768,384]{1,0:T(8,128)}, f32[768,384]{1,0:T(8,128)}, f32[768,384]{1,0:T(8,128)}, f32[384,768]{1,0:T(8,128)}, f32[768,1536]{1,0:T(8,128)}, /*index=5*/f32[1536,768]{1,0:T(8,128)}) async-done(((f32[768,384]{1,0:T(8,128)}, f32[768,384]{1,0:T(8,128)}, f32[768,384]{1,0:T(8,128)}, f32[384,768]{1,0:T(8,128)}, f32[768,1536]{1,0:T(8,128)}, /*index=5*/f32[1536,768]{1,0:T(8,128)}), ...) | async-done | bytes 14155792 | tf_op jit(solution)/shard_map/psum | solution.py:263
  (288 shorter events, 119.1 us)
Async XLA Ops:
  7.2 101.5 %copy-start = (bf16[1536,768]{1,0:T(8,128)(2,1)S(1)}, bf16[1536,768]{1,0:T(8,128)(2,1)}, u32[]{:S(2)}) copy-start(bf16[1536,768]{1,0:T(8,128)(2,1)} %param.39) | copy-start | bytes 7077892
  7.2 18.2 %all-gather.5.cloned.1.call-start = ((), (), s32[]{:S(2)}) async-start(), calls=%async_computation.4 | async-start | bytes 2359296 | tf_op jit(solution)/shard_map/all_gather | solution.py:168
  12.8 66.2 %reduce-scatter.5.cloned.1.call-start = ((), (), s32[]{:S(2)}) async-start(), calls=%async_computation.5 | async-start | bytes 4718592 | tf_op jit(solution)/shard_map/reduce_scatter | solution.py:182
  66.8 28.9 %all-gather.7.cloned.1.call-start = ((), (), s32[]{:S(2)}) async-start(), calls=%async_computation.6 | async-start | bytes 2359296 | tf_op jit(solution)/shard_map/all_gather | solution.py:192
  84.5 24.2 %all-gather.9.cloned.1.call-start = ((), (), s32[]{:S(2)}) async-start(), calls=%async_computation.8 | async-start | bytes 2359296 | tf_op jit(solution)/shard_map/all_gather | solution.py:206
  85.1 52.5 %reduce-scatter.9.cloned.1.call-start = ((), (), s32[]{:S(2)}) async-start(), calls=%async_computation.9 | async-start | bytes 4718592 | tf_op jit(solution)/shard_map/reduce_scatter | solution.py:212
  108.7 12.4 %copy-start.69 = (bf16[768,1536]{1,0:T(8,128)(2,1)S(1)}, bf16[768,1536]{1,0:T(8,128)(2,1)}, u32[]{:S(2)}) copy-start(bf16[768,1536]{1,0:T(8,128)(2,1)} %param.37) | copy-start | bytes 7077892
  125.4 24.6 %reduce-scatter.7.cloned.1.call-start = ((), (), s32[]{:S(2)}) async-start(), calls=%async_computation.7 | async-start | bytes 2359296 | tf_op jit(solution)/shard_map/reduce_scatter | solution.py:198
  131.2 6.5 copy-start.6
  131.2 35.7 %all-gather.11.cloned.1.call-start = ((), (), s32[]{:S(2)}) async-start(), calls=%async_computation.10 | async-start | bytes 2359296 | tf_op jit(solution)/shard_map/all_gather | solution.py:217
  140.2 14.2 %copy-start.18 = (bf16[512,768]{1,0:T(8,128)(2,1)S(1)}, bf16[512,768]{1,0:T(8,128)(2,1)}, u32[]{:S(2)}) copy-start(bf16[512,768]{1,0:T(8,128)(2,1)} %param.41) | copy-start | bytes 2359300
  155.7 192.2 %reduce-scatter.11.cloned.1.call-start = ((), (), s32[]{:S(2)}) async-start(), calls=%async_computation.11 | async-start | bytes 4718592 | tf_op jit(solution)/shard_map/reduce_scatter | solution.py:238
  155.8 15.3 %copy-start.9 = (bf16[1024,6,64]{0,2,1:T(8,128)(2,1)S(1)}, bf16[1024,6,64]{0,2,1:T(8,128)(2,1)}, u32[]{:S(2)}) copy-start(bf16[1024,6,64]{0,2,1:T(8,128)(2,1)} %get-tuple-element.530) | copy-start | bytes 2359300
  190.9 6.0 copy-start.2
  241.4 7.9 %copy-start.24 = (bf16[1024,1536]{1,0:T(8,128)(2,1)S(1)}, bf16[1024,1536]{1,0:T(8,128)(2,1)}, u32[]{:S(2)}) copy-start(bf16[1024,1536]{1,0:T(8,128)(2,1)} %copy-done.23) | copy-start | bytes 9437188
  241.4 423.4 %all-reduce.5.cloned.1.call-start = ((), (), s32[]{:S(2)}) async-start(), calls=%async_computation.12 | async-start | bytes 28311552 | tf_op jit(solution)/shard_map/psum | solution.py:263
  241.7 7.6 %copy-start.33 = (bf16[1024,768]{1,0:T(8,128)(2,1)S(1)}, bf16[1024,768]{1,0:T(8,128)(2,1)}, u32[]{:S(2)}) copy-start(bf16[1024,768]{1,0:T(8,128)(2,1)} %all-gather.7.cloned.1.call-done) | copy-start | bytes 4718596
  264.1 83.7 %copy-start.8 = (bf16[512,768]{1,0:T(8,128)(2,1)S(1)}, bf16[512,768]{1,0:T(8,128)(2,1)}, u32[]{:S(2)}) copy-start(bf16[512,768]{1,0:T(8,128)(2,1)} %param.23) | copy-start | bytes 2359300
  264.1 83.7 %copy-start.46 = (f32[768]{0:T(1024)S(1)}, f32[768]{0:T(1024)}, u32[]{:S(2)}) copy-start(f32[768]{0:T(1024)} %copy-done.45) | copy-start | bytes 9220
  264.1 83.7 %copy-start.48 = (f32[512]{0:T(512)S(1)}, f32[512]{0:T(512)}, u32[]{:S(2)}) copy-start(f32[512]{0:T(512)} %copy-done.47) | copy-start | bytes 6148
  266.2 84.0 %copy-start.54 = (f32[512]{0:T(512)S(1)}, f32[512]{0:T(512)}, u32[]{:S(2)}) copy-start(f32[512]{0:T(512)} %copy-done.53) | copy-start | bytes 6148
  266.2 84.0 %copy-start.50 = (f32[512]{0:T(512)S(1)}, f32[512]{0:T(512)}, u32[]{:S(2)}) copy-start(f32[512]{0:T(512)} %copy-done.49) | copy-start | bytes 6148
  350.1 41.5 %copy-start.19 = (bf16[512,768]{1,0:T(8,128)(2,1)S(1)}, bf16[512,768]{1,0:T(8,128)(2,1)}, u32[]{:S(2)}) copy-start(bf16[512,768]{1,0:T(8,128)(2,1)} %param.41) | copy-start | bytes 2359300
  350.2 41.4 %copy-start.52 = (f32[512]{0:T(512)S(1)}, f32[512]{0:T(512)}, u32[]{:S(2)}) copy-start(f32[512]{0:T(512)} %copy-done.51) | copy-start | bytes 6148
  (67 other events, 162.0 us)
Sparse Core Ops, SparseCore 0:
  12.9 12.4 all-gather.4
  66.9 12.0 reduce-scatter.4
  84.6 10.9 all-gather.6
  97.7 10.9 all-gather.8
  125.5 12.0 reduce-scatter.8
  139.7 10.2 reduce-scatter.6
  155.8 10.9 all-gather.10
  241.5 12.0 reduce-scatter.10
  261.7 402.9 all-reduce.4
where the time goes:
time: 693 us; the launch traced here: 684 us
  waiting for transfers between devices  337 us (49%)
  matrix products  122 us (18%)
  blocking collectives  122 us (18%)
  other arithmetic  46.5 us (7%)
  local copies, waits for them, and re-layouts  33.5 us (5%)
  between operations  14.9 us (2%)
  loops' own time  7.13 us (1%)
    psum x1, waiting for transfers between devices, on_device(): lax.psum((expand_weight_grad, expand_bias_grad, contract_weight_grad, con...  270 us
    psum x1, blocking collectives, on_device(): lax.psum((expand_weight_grad, expand_bias_grad, contract_weight_grad, con...  81.7 us
    psum x1, blocking collectives, on_device(): lax.psum((gain_first_grad, shift_first_grad, gain_second_grad, shift_seco...  40.6 us
    unnamed x140, local copies, waits for them, and re-layouts  24.2 us
    dot_general x4, matrix products, masked_scores(): jnp.einsum('qhd,khd->hqk', query_block, keys, preferred_element_type=jnp....  23.3 us
    dot_general x6, matrix products, transposed_product(): lax.dot_general(left, right, (((1,), (1,)), ((), ())), preferred_element_...  23 us
    dot_general x6, matrix products, rows_product(): lax.dot_general(left, right, (((0,), (0,)), ((), ())), preferred_element_...  19.9 us
    dot_general x2, matrix products, one(): jnp.einsum('qhd,khd->hqk', grad_block, values, preferred_element_type=jnp...  15.2 us
  transfers between devices with their start and end apart: 9, of which 8 were waited for; matrix products, arithmetic and copies ran while one was open for 6% of the time, Pallas kernels for 0%

commit v1 on v0

v1 whole, which is shorter than its diff:
```python
import functools

import jax
import jax.numpy as jnp
from jax import lax
from jax.experimental import pallas as pl
from jax.experimental.pallas import tpu as pltpu
from jax.sharding import PartitionSpec as P

HD = 64


epsilon = 1e-05


def layer_norm(values, gain, shift):
    average = jnp.mean(values, axis=-1, keepdims=True)
    centred = values - average
    variance = jnp.mean(centred * centred, axis=-1, keepdims=True)
    return centred * lax.rsqrt(variance + epsilon) * gain + shift


def gelu_tanh(values):
    return jax.nn.gelu(values, approximate=True)


def row_segments(lengths, owners, group, total_rows):
    count = lengths.shape[0]
    index = jnp.arange(count, dtype=jnp.int32)
    same = owners[None, :] == owners[:, None]
    earlier = index[None, :] < index[:, None]
    starts = jnp.sum(jnp.where(same & earlier, lengths[None, :], 0), axis=1, dtype=jnp.int32)
    positions = jnp.arange(total_rows, dtype=jnp.int32)[:, None]
    inside = (
        (owners[None, :] == group)
        & (positions >= starts[None, :])
        & (positions < starts[None, :] + lengths[None, :])
    )
    segments = jnp.sum(jnp.where(inside, index[None, :] + 1, 0), axis=1, dtype=jnp.int32)
    used = jnp.sum(jnp.where(owners == group, lengths, 0), dtype=jnp.int32)
    first = jnp.sum(jnp.where(inside, starts[None, :], 0), axis=1, dtype=jnp.int32)
    return segments, jnp.where(segments > 0, first, used)


def rows_product(left, right):
    return lax.dot_general(
        left, right, (((0,), (0,)), ((), ())), preferred_element_type=jnp.float32
    )


def transposed_product(left, right):
    return lax.dot_general(
        left, right, (((1,), (1,)), ((), ())), preferred_element_type=jnp.float32
    )


QB = 256
MASKED = -1e30


def heads_dot(left, right, left_dim, right_dim):
    return lax.dot_general(
        left, right, (((left_dim,), (right_dim,)), ((), ())), preferred_element_type=jnp.float32
    )


def fill_mask(first_ref, mask_ref):
    total = mask_ref.shape[0]
    for start in range(0, total, QB):
        rows = start + lax.broadcasted_iota(jnp.int32, (QB, total), 0)
        columns = lax.broadcasted_iota(jnp.int32, (QB, total), 1)
        allowed = (columns >= first_ref[start : start + QB, :]) & (columns <= rows)
        mask_ref[start : start + QB, :] = jnp.where(allowed, 0.0, MASKED)


def forward_kernel(first_ref, query_ref, keys_ref, values_ref, mixed_ref, log_ref, mask_ref):
    @pl.when(pl.program_id(0) == 0)
    def _():
        fill_mask(first_ref, mask_ref)

    total = query_ref.shape[0]
    for start in range(0, total, QB):
        stop = start + QB
        outs, logs = [], []
        for h in range(2):
            lanes = slice(h * HD, (h + 1) * HD)
            scores = heads_dot(query_ref[start:stop, lanes], keys_ref[:stop, lanes], 1, 1)
            scores = scores + mask_ref[start:stop, :stop]
            top = jnp.max(scores, axis=-1, keepdims=True)
            powers = jnp.exp(scores - top)
            sums = jnp.sum(powers, axis=-1, keepdims=True)
            probs = (powers * (1.0 / sums)).astype(jnp.bfloat16)
            outs.append(heads_dot(probs, values_ref[:stop, lanes], 1, 0))
            logs.append(jnp.broadcast_to(top + jnp.log(sums), (QB, HD)))
        mixed_ref[start:stop, :] = jnp.concatenate(outs, axis=1).astype(jnp.bfloat16)
        log_ref[start:stop, :] = jnp.concatenate(logs, axis=1)


def backward_kernel(
    first_ref, query_ref, keys_ref, values_ref, log_ref, grad_ref,
    grad_query_ref, grad_keys_ref, grad_values_ref, mask_ref, keys_sum, values_sum,
):
    @pl.when(pl.program_id(0) == 0)
    def _():
        fill_mask(first_ref, mask_ref)

    total = query_ref.shape[0]
    for start in range(total - QB, -1, -QB):
        stop = start + QB
        parts = ([], [], [])
        for h in range(2):
            lanes = slice(h * HD, (h + 1) * HD)
            query = query_ref[start:stop, lanes]
            grad = grad_ref[start:stop, lanes]
            keys = keys_ref[:stop, lanes]
            scores = heads_dot(query, keys, 1, 1) + mask_ref[start:stop, :stop]
            probs = jnp.exp(scores - log_ref[start:stop, h * HD : h * HD + 1])
            grad_probs = heads_dot(grad, values_ref[:stop, lanes], 1, 1)
            inner = jnp.sum(probs * grad_probs, axis=-1, keepdims=True)
            grad_scores = (probs * (grad_probs - inner)).astype(jnp.bfloat16)
            parts[0].append(heads_dot(grad_scores, keys, 1, 0))
            parts[1].append(heads_dot(grad_scores, query, 0, 0))
            parts[2].append(heads_dot(probs.astype(jnp.bfloat16), grad, 0, 0))
        grad_query_ref[start:stop, :] = (
            jnp.concatenate(parts[0], axis=1) * (HD ** (-0.5))
        ).astype(jnp.bfloat16)
        for sums, part in ((keys_sum, parts[1]), (values_sum, parts[2])):
            part = jnp.concatenate(part, axis=1)
            if stop == total:
                sums[...] = part
            else:
                sums[:stop, :] += part
    grad_keys_ref[...] = keys_sum[...].astype(jnp.bfloat16)
    grad_values_ref[...] = values_sum[...].astype(jnp.bfloat16)


def attention_call(kernel, out_types, scratch, flops, name, first, *operands):
    rows, width = operands[0].shape
    pair = pl.BlockSpec((rows, 2 * HD), lambda i: (0, i))
    return pl.pallas_call(
        kernel,
        grid=(width // (2 * HD),),
        in_specs=[pl.BlockSpec((rows, 1), lambda i: (0, 0))] + [pair] * len(operands),
        out_specs=[pair] * len(out_types),
        out_shape=[jax.ShapeDtypeStruct((rows, width), kind) for kind in out_types],
        scratch_shapes=[pltpu.VMEM((rows, rows), jnp.float32)]
        + [pltpu.VMEM((rows, 2 * HD), jnp.float32)] * scratch,
        compiler_params=pltpu.CompilerParams(vmem_limit_bytes=40 * 1024 * 1024),
        cost_estimate=pl.CostEstimate(
            flops=flops, bytes_accessed=8 * rows * width * 2, transcendentals=rows * rows * 4
        ),
        name=name,
    )(first, *operands)


def swap(values):
    return lax.ppermute(values, "tensor", [(0, 1), (1, 0)])


def sum_kernel(groups, orders, chains, count, *refs):
    inputs, outputs = refs[:count], refs[count : 2 * count]
    works, arrived = refs[2 * count : 3 * count], refs[3 * count : 4 * count]
    send_sem, recv_sem = refs[4 * count :]
    group = lax.axis_index("dp")
    steps = len(orders[0])
    digit = [(group // (1 << bit)) % 2 for bit in range(steps)]
    partner = [group + (1 - 2 * digit[bit]) * (1 << bit) for bit in range(steps)]

    barrier = pltpu.get_barrier_semaphore()
    for bit in range(steps):
        pl.semaphore_signal(
            barrier, inc=1, device_id={"dp": partner[bit]}, device_id_type=pl.DeviceIdType.MESH
        )
    pl.semaphore_wait(barrier, steps)

    def copy(chain, step, bit, source, target):
        slot = chain * 2 * steps + step
        made = pltpu.make_async_remote_copy(
            src_ref=source,
            dst_ref=target,
            send_sem=send_sem.at[slot],
            recv_sem=recv_sem.at[slot],
            device_id={"dp": partner[bit]},
            device_id_type=pl.DeviceIdType.MESH,
        )
        made.start()
        return made

    def rows_at(start, size):
        return pl.ds(pl.multiple_of(start, 16), size)

    offsets = [[0] for _ in chains]
    pending = [None for _ in chains]
    started = []

    def scatter_start(c, step):
        array, low, high, kind = chains[c]
        rows = inputs[array].shape[0]
        half = rows >> (step + 1)
        bit = orders[kind][step]
        source = inputs[array] if step == 0 else works[array]
        sent = offsets[c][-1] + (1 - digit[bit]) * half
        pending[c] = copy(
            c, step, bit,
            source.at[rows_at(sent, half), low:high],
            arrived[array].at[rows - 2 * half : rows - half, low:high],
        )
        started.append(pending[c])
        offsets[c].append(offsets[c][-1] + digit[bit] * half)

    def scatter_add(c, step):
        array, low, high, kind = chains[c]
        rows = inputs[array].shape[0]
        half = rows >> (step + 1)
        kept = offsets[c][-1]
        pending[c].wait_recv()
        tile = 48 if half % 48 == 0 else 16
        source = inputs[array] if step == 0 else works[array]
        target = outputs[array] if step == steps - 1 else works[array]

        def add(i, carry):
            here = rows_at(kept + i * tile, tile)
            there = rows_at(rows - 2 * half + i * tile, tile)
            total = source[here, low:high].astype(jnp.float32) + arrived[array][
                there, low:high
            ].astype(jnp.float32)
            target[here, low:high] = total.astype(jnp.bfloat16)
            return carry

        lax.fori_loop(0, half // tile, add, 0)

    def gather_start(c, step):
        array, low, high, kind = chains[c]
        size = inputs[array].shape[0] >> step
        block = outputs[array].at[rows_at(offsets[c][step], size), low:high]
        pending[c] = copy(c, 2 * steps - step, orders[kind][step - 1], block, block)
        started.append(pending[c])

    every = range(len(chains))
    for c in every:
        scatter_start(c, 0)
    for step in range(steps):
        for c in every:
            scatter_add(c, step)
            if step < steps - 1:
                scatter_start(c, step + 1)
            else:
                gather_start(c, steps)
    for step in range(steps - 1, 0, -1):
        for c in every:
            pending[c].wait_recv()
            gather_start(c, step)
    for c in every:
        pending[c].wait_recv()
    for made in started:
        made.wait_send()


def sum_over_groups(arrays, groups):
    if any(array.shape[0] % (16 * groups) for array in arrays):
        return lax.psum(tuple(arrays), "dp")
    bits = list(range(groups.bit_length() - 1))
    orders = (bits, bits[1:2] + bits[:1] + bits[2:], bits[2:] + bits[:2])
    chains = []
    for index, array in enumerate(arrays):
        width = array.shape[1]
        if index == 0:
            cuts = [(0, width // 2, 0), (width // 2, width, 1)]
        elif index in (1, 2):
            third = width // 3
            cuts = [(i * third, (i + 1) * third, i) for i in range(3)]
        else:
            cuts = [(0, width, index - 3)]
        chains += [(index,) + cut for cut in cuts]
    count = len(arrays)
    slots = len(chains) * 2 * len(bits)
    shapes = [jax.ShapeDtypeStruct(array.shape, array.dtype) for array in arrays]
    buffers = [pltpu.VMEM(array.shape, array.dtype) for array in arrays]
    vmem = pl.BlockSpec(memory_space=pltpu.VMEM)
    return pl.pallas_call(
        functools.partial(sum_kernel, groups, orders, chains, count),
        out_shape=shapes,
        in_specs=[vmem] * count,
        out_specs=[vmem] * count,
        scratch_shapes=buffers
        + buffers
        + [pltpu.SemaphoreType.DMA((slots,)), pltpu.SemaphoreType.DMA((slots,))],
        compiler_params=pltpu.CompilerParams(
            collective_id=0, has_side_effects=True, vmem_limit_bytes=48 * 1024 * 1024
        ),
        name="sum_over_groups",
    )(*arrays)


def on_device(
    tokens,
    lengths,
    owners,
    gain_first,
    shift_first,
    query_weight,
    key_weight,
    value_weight,
    query_bias,
    value_bias,
    output_weight,
    output_bias,
    gain_second,
    shift_second,
    expand_weight,
    expand_bias,
    contract_weight,
    contract_bias,
    cotangent,
):
    own_rows = tokens.shape[0]
    group = lax.axis_index("dp")
    side = lax.axis_index("tensor")
    first_row = side * own_rows
    other_row = (1 - side) * own_rows

    def in_order(own, other):
        return jnp.concatenate(
            [jnp.where(side == 0, own, other), jnp.where(side == 0, other, own)], axis=0
        )

    def halves(values):
        return (
            lax.dynamic_slice_in_dim(values, first_row, own_rows, 0),
            lax.dynamic_slice_in_dim(values, other_row, own_rows, 0),
        )

    segments, firsts = row_segments(lengths, owners, group, 2 * own_rows)
    firsts = firsts[:, None]
    own_segments = lax.dynamic_slice_in_dim(segments, first_row, own_rows, 0)
    live = (own_segments > 0).astype(jnp.float32)[:, None]
    scale = HD ** (-0.5)
    width = query_weight.shape[1]
    upstream = cotangent.astype(jnp.float32)
    own_two = (live * upstream).astype(jnp.bfloat16)
    inputs = tokens.astype(jnp.float32)
    normed_value, pull_first = jax.vjp(
        layer_norm, inputs, gain_first.astype(jnp.float32), shift_first.astype(jnp.float32)
    )
    own_normed = normed_value.astype(jnp.bfloat16)
    normed = in_order(own_normed, swap(own_normed))
    grad_two = jnp.concatenate([own_two, swap(own_two)], axis=0)
    query = (
        jnp.dot(normed, query_weight, preferred_element_type=jnp.float32)
        + query_bias.astype(jnp.float32)
    ).astype(jnp.bfloat16) * jnp.bfloat16(scale)
    keys = jnp.dot(normed, key_weight, preferred_element_type=jnp.float32).astype(jnp.bfloat16)
    values = (
        jnp.dot(normed, value_weight, preferred_element_type=jnp.float32)
        + value_bias.astype(jnp.float32)
    ).astype(jnp.bfloat16)
    pairs = 2 * own_rows * 2 * own_rows * width
    mixed, logs = attention_call(
        forward_kernel, (jnp.bfloat16, jnp.float32), 0, 3 * pairs, "attend",
        firsts, query, keys, values,
    )

    def summed(product, values, send_type=jnp.bfloat16):
        own, other = values
        received = swap(product(other).astype(send_type))
        return product(own) + received.astype(jnp.float32)

    branch = summed(
        lambda rows: jnp.dot(rows, output_weight, preferred_element_type=jnp.float32),
        halves(mixed),
    ) + output_bias.astype(jnp.float32)
    hidden = inputs + live * branch
    middle_value, pull_second = jax.vjp(
        layer_norm, hidden, gain_second.astype(jnp.float32), shift_second.astype(jnp.float32)
    )
    own_middle = middle_value.astype(jnp.bfloat16)
    middle = jnp.concatenate([own_middle, swap(own_middle)], axis=0)
    before = jnp.dot(
        middle, expand_weight, preferred_element_type=jnp.float32
    ) + expand_bias.astype(jnp.float32)
    active_value, pull_active = jax.vjp(gelu_tanh, before)
    active = active_value.astype(jnp.bfloat16)
    contract_weight_grad = rows_product(active, grad_two).astype(jnp.bfloat16)
    contract_bias_grad = jnp.sum(grad_two, axis=0, dtype=jnp.float32)
    grad_before = pull_active(transposed_product(grad_two, contract_weight))[0].astype(jnp.bfloat16)
    expand_weight_grad = rows_product(middle, grad_before).astype(jnp.bfloat16)
    expand_bias_grad = jnp.sum(grad_before, axis=0, dtype=jnp.float32)
    grad_middle = summed(
        lambda rows: transposed_product(rows, expand_weight),
        (grad_before[:own_rows], grad_before[own_rows:]),
    )
    branch_two = summed(
        lambda rows: jnp.dot(rows, contract_weight, preferred_element_type=jnp.float32),
        (active[:own_rows], active[own_rows:]),
    ) + contract_bias.astype(jnp.float32)
    result = (hidden + live * branch_two).astype(jnp.bfloat16)
    grad_norm_two, gain_second_grad, shift_second_grad = pull_second(grad_middle)
    grad_hidden = upstream + grad_norm_two
    own_branch = (live * grad_hidden).astype(jnp.bfloat16)
    grad_branch = in_order(own_branch, swap(own_branch))
    output_weight_grad = rows_product(grad_branch, mixed)
    output_bias_grad = jnp.sum(grad_branch, axis=0, dtype=jnp.float32)
    grad_mixed = transposed_product(grad_branch, output_weight).astype(jnp.bfloat16)
    grad_query, grad_keys, grad_values = attention_call(
        backward_kernel, (jnp.bfloat16,) * 3, 2, 6 * pairs, "attend_back",
        firsts, query, keys, values, logs, grad_mixed,
    )
    query_weight_grad = rows_product(normed, grad_query)
    key_weight_grad = rows_product(normed, grad_keys)
    value_weight_grad = rows_product(normed, grad_values)
    query_bias_grad = jnp.sum(grad_query, axis=0, dtype=jnp.float32)
    value_bias_grad = jnp.sum(grad_values, axis=0, dtype=jnp.float32)
    query_rows, keys_rows, values_rows = halves(grad_query), halves(grad_keys), halves(grad_values)
    grad_normed = summed(
        lambda rows: transposed_product(rows[0], query_weight)
        + transposed_product(rows[1], key_weight)
        + transposed_product(rows[2], value_weight),
        tuple(zip(query_rows, keys_rows, values_rows)),
    )
    grad_norm_one, gain_first_grad, shift_first_grad = pull_first(grad_normed)
    tokens_grad = (grad_hidden + grad_norm_one).astype(jnp.bfloat16)
    norms = jnp.stack([gain_first_grad, shift_first_grad, gain_second_grad, shift_second_grad])
    norms = norms + swap(norms)
    small = (
        norms, query_bias_grad, value_bias_grad, output_bias_grad, expand_bias_grad,
        contract_bias_grad,
    )
    small = jnp.concatenate([item.reshape(-1, width) for item in small], axis=0)
    small_rows = small.shape[0]
    small = jnp.pad(small, ((0, -small_rows % 256), (0, 0)))
    depth = query_weight.shape[0]
    packed = jnp.concatenate([value_weight_grad, small], axis=0).astype(jnp.bfloat16)
    (
        contract_weight_grad,
        expand_weight_grad,
        output_weight_grad,
        query_weight_grad,
        key_weight_grad,
        packed,
    ) = sum_over_groups(
        (
            contract_weight_grad,
            expand_weight_grad,
            output_weight_grad.astype(jnp.bfloat16),
            query_weight_grad.astype(jnp.bfloat16),
            key_weight_grad.astype(jnp.bfloat16),
            packed,
        ),
        lax.axis_size("dp"),
    )
    packed = packed.astype(jnp.float32)
    value_weight_grad = packed[:depth]
    small = packed[depth : depth + small_rows].reshape(-1)
    features = gain_first.shape[0]
    sizes = (features,) * 4 + (width, width, features, expand_bias.shape[0], features)
    cuts, at = [], 0
    for size in sizes:
        cuts.append(small[at : at + size])
        at += size
    gain_first_grad, shift_first_grad, gain_second_grad, shift_second_grad = cuts[:4]
    query_bias_grad, value_bias_grad, output_bias_grad = cuts[4:7]
    expand_bias_grad, contract_bias_grad = cuts[7:]
    key_weight_grad = key_weight_grad.astype(jnp.float32)
    query_weight_grad = query_weight_grad.astype(jnp.float32)
    output_weight_grad = output_weight_grad.astype(jnp.float32).T
    expand_weight_grad = expand_weight_grad.astype(jnp.float32)
    contract_weight_grad = contract_weight_grad.astype(jnp.float32)
    return (
        result,
        tokens_grad,
        gain_first_grad,
        shift_first_grad,
        query_weight_grad,
        key_weight_grad,
        value_weight_grad,
        query_bias_grad,
        value_bias_grad,
        output_weight_grad,
        output_bias_grad,
        gain_second_grad,
        shift_second_grad,
        expand_weight_grad,
        expand_bias_grad,
        contract_weight_grad,
        contract_bias_grad,
    )


def solution(mesh):
    in_specs = (
        P(("dp", "tensor"), None),
        P(),
        P(),
        P(),
        P(),
        P(None, "tensor"),
        P(None, "tensor"),
        P(None, "tensor"),
        P("tensor"),
        P("tensor"),
        P("tensor", None),
        P(),
        P(),
        P(),
        P(None, "tensor"),
        P("tensor"),
        P("tensor", None),
        P(),
        P(("dp", "tensor"), None),
    )
    out_specs = (
        P(("dp", "tensor"), None),
        P(("dp", "tensor"), None),
        P(),
        P(),
        P(None, "tensor"),
        P(None, "tensor"),
        P(None, "tensor"),
        P("tensor"),
        P("tensor"),
        P("tensor", None),
        P(),
        P(),
        P(),
        P(None, "tensor"),
        P("tensor"),
        P("tensor", None),
        P(),
    )
    return jax.shard_map(
        on_device, mesh=mesh, in_specs=in_specs, out_specs=out_specs, check_vma=False
    )
```

time: 693 us -> 290 us (0.42)
  waiting for transfers between devices: 337 us -> 3.89 us
  Pallas kernels: 0 us -> 177 us
  blocking collectives: 122 us -> 0 us
  matrix products: 122 us -> 58 us
  other arithmetic: 46.5 us -> 23.7 us
  local copies, waits for them, and re-layouts: 33.5 us -> 19.7 us
  between operations: 14.9 us -> 1.69 us
  loops' own time: 7.13 us -> 0 us
    psum x1 -> x0, waiting for transfers between devices: 270 us -> none  [on_device(): lax.psum((expand_weight_grad, expand_bias_grad, contract_weight_grad, con...]
    pallas_call x0 -> x3, Pallas kernels: none -> 177 us  [the longest x1 143 us: sum_over_groups(): pl.pallas_call(functools.partial(sum_kernel, groups, orders, chains, coun...]
    psum x2 -> x0, blocking collectives: 122 us -> none  [the longest x1 81.7 us: on_device(): lax.psum((expand_weight_grad, expand_bias_grad, contract_weight_grad, con...]
    dot_general x16 -> x4, matrix products: 65.5 us -> 10 us  [the longest x2 6.29 us: on_device(): jnp.dot(rows, contract_weight, preferred_element_type=jnp.float32)]
    all_gather x4 -> x0, waiting for transfers between devices: 39.4 us -> none  [the longest x1 12.2 us: on_device(): lax.all_gather(normed_value.astype(jnp.bfloat16), 'tensor', axis=0, tiled...]
    reduce_scatter x4 -> x0, waiting for transfers between devices: 27 us -> none  [the longest x1 11.5 us: on_device(): lax.psum_scatter(jnp.dot(mixed, output_weight, preferred_element_type=jnp...]
    unnamed x140 -> x149, local copies, waits for them, and re-layouts: 24.2 us -> 11.2 us
    reduce_sum x3 -> x1, other arithmetic: 10.6 us -> 0.64 us  [row_segments(): used = jnp.sum(jnp.where(owners == group, lengths, 0), dtype=jnp.int32)]
  transfers between devices with their start and end apart: 9 -> 9, of which waited for: 8 -> 2; matrix products, arithmetic and copies ran while one was open for 6% -> 10% of each run, Pallas kernels for 0% -> 0%
where the time goes in v1:
time: 290 us; the launch traced here: 286 us
  Pallas kernels  177 us (61%)
  matrix products  58 us (20%)
  other arithmetic  23.7 us (8%)
  local copies, waits for them, and re-layouts  19.7 us (7%)
  waiting for transfers between devices  3.89 us (1%)
    pallas_call x1, Pallas kernels, sum_over_groups(): pl.pallas_call(functools.partial(sum_kernel, groups, orders, chains, coun...  143 us
    pallas_call x2, Pallas kernels, attention_call(): pl.pallas_call(kernel, grid=(width // (2 * HD),), in_specs=[pl.BlockSpec(...  33.4 us
    dot_general x10, matrix products, transposed_product(): lax.dot_general(left, right, (((1,), (1,)), ((), ())), preferred_element_...  24.4 us
    dot_general x6, matrix products, rows_product(): lax.dot_general(left, right, (((0,), (0,)), ((), ())), preferred_element_...  17 us
    unnamed x149, local copies, waits for them, and re-layouts  11.2 us
    dot_general x2, matrix products, on_device(): jnp.dot(rows, contract_weight, preferred_element_type=jnp.float32)  6.29 us
    slice x10, local copies, waits for them, and re-layouts, on_device(): cuts.append(small[at:at + size])  6.18 us
  transfers between devices with their start and end apart: 9, of which 2 were waited for; matrix products, arithmetic and copies ran while one was open for 10% of the time, Pallas kernels for 0%

profile of v1, /device:TPU:0, one launch (start us, length us, event | category | flops | bytes accessed | tf_op | source)
XLA Modules:
  0.0 285.9 jit_solution(6039997986618437643)
XLA Ops:
  8.2 1.7 broadcast_select_fusion.3
  14.1 13.9 %attend.1 = (bf16[1024,384]{1,0:T(8,128)(2,1)S(1)}, f32[1024,384]{1,0:T(8,128)S(1)}) custom-call(s32[1024,1]{1,0:T(8,128)S(1)} %copy-done.5, bf16[1024,384]{1,0:T(8,128)(2,1)S(1)} %fusion.34.query_ref, bf16[1024,384]{1,0:T(8,128)(2,1)S(1)} %convolution_convert_fusion.3.keys_ref, bf16[1024,384]{1,0:T(8,128)(2,1)S(1)} %add_convert_fusion.4.values_ref), custom_call_target="tpu_custom_call" | custom-call | flops 1207959552 | bytes 6291456 | tf_op jit(solution)/shard_map/attend/pallas_call | solution.py:140
  30.8 2.4 collective-permute-done.1
  33.3 2.3 fusion.81
  39.4 3.7 %multiply_convert_fusion = (bf16[1024,1536]{1,0:T(8,128)(2,1)S(1)}, f32[1024,1536]{1,0:T(8,128)S(1)}) fusion(f32[1536]{0:T(1024)S(1)} %convert_element_type.161, bf16[768,1536]{1,0:T(8,128)(2,1)S(1)} %copy-done, bf16[512,768]{1,0:T(8,128)(2,1)S(1)} %collective-permute-done.2, bf16[512,768]{1,0:T(8,128)(2,1)S(1)} %add_convert_fusion.3), kind=kOutput, calls=%fused_computation.9 | convolution fusion | flops 2434793472 | bytes 13375488 | tf_op jit(solution)/shard_map/dot_general | solution.py:378
  43.2 7.4 %fusion.82 = (bf16[1536]{0:T(1024)(128)(2,1)S(1)}, bf16[1024,1536]{1,0:T(8,128)(2,1)S(1)}) fusion(f32[1024,1536]{1,0:T(8,128)S(1)} %get-tuple-element.126, f32[1536]{0:T(1024)S(1)} %convert_element_type.161, bf16[1536,768]{1,0:T(8,128)(2,1)S(1)} %copy-done.66, bf16[512,768]{1,0:T(8,128)(2,1)S(1)} %collective-permute-done.4, ...), kind=kOutput, calls=%fused_computation.139 | convolution fusion | flops 2453666304 | bytes 13378560 | tf_op jit(solution)/shard_map/dot_general | solution.py:52
  50.6 2.3 fusion.31
  53.1 2.3 fusion.28
  57.1 4.0 %multiply_reduce_fusion = (f32[768]{0:T(1024)S(1)}, f32[512]{0:T(512)S(1)}, f32[768]{0:T(1024)S(1)}, f32[512,768]{1,0:T(8,128)S(1)}) fusion(f32[512,768]{1,0:T(8,128)} %copy-done.17, f32[512]{0:T(512)S(1)} %fusion.67, f32[512]{0:T(512)S(1)} %broadcast_multiply_fusion, bf16[512,768]{1,0:T(8,128)(2,1)} %collective-permute-done.5, ...), kind=kOutput, calls=%fused_computation.44 | convolution fusion | flops 1211889664 | bytes 7879680 | tf_op jit(solution)/shard_map/dot_general | solution.py:52
  61.3 4.0 %fusion.79 = (f32[512]{0:T(512)S(1)}, f32[512,768]{1,0:T(8,128)S(1)}, bf16[512,768]{1,0:T(8,128)(2,1)}) fusion(f32[512]{0:T(512)S(1)} %multiply_multiply_fusion.3, f32[512,768]{1,0:T(8,128)S(1)} %copy-done.18, f32[512]{0:T(512)S(1)} %broadcast_multiply_fusion, f32[512]{0:T(512)S(1)} %fusion.67, f32[768]{0:T(1024)S(1)} %convert_element_type.158, ...), kind=kOutput, calls=%fused_computation.136 | convolution fusion | flops 1213857280 | bytes 11028480 | tf_op jit(solution)/shard_map/dot_general | solution.py:393
  67.3 3.9 %convolution_convert_fusion.refs_1_ = bf16[768,1536]{1,0:T(8,128)(2,1)} fusion(bf16[1024,1536]{1,0:T(8,128)(2,1)S(1)} %copy-done.71, bf16[512,768]{1,0:T(8,128)(2,1)S(1)} %copy-done.69, bf16[512,768]{1,0:T(8,128)(2,1)S(1)} %copy-done.45), kind=kOutput, calls=%fused_computation.10 | convolution fusion | flops 2420244480 | bytes 7077888 | tf_op jit(solution)/shard_map/dot_general | solution.py:46
  71.2 6.0 %convolution_convert_fusion.1.refs_0_ = bf16[1536,768]{1,0:T(8,128)(2,1)} fusion(bf16[1024,1536]{1,0:T(8,128)(2,1)} %copy-done.72, bf16[512,768]{1,0:T(8,128)(2,1)S(1)} %copy-done.39, bf16[512,768]{1,0:T(8,128)(2,1)S(1)} %copy-done.37), kind=kOutput, calls=%fused_computation.11 | convolution fusion | flops 2420244480 | bytes 7077888 | tf_op jit(solution)/shard_map/dot_general | solution.py:46
  77.2 1.6 fusion.78
  81.6 19.5 %attend_back.1 = (bf16[1024,384]{1,0:T(8,128)(2,1)S(1)}, bf16[1024,384]{1,0:T(8,128)(2,1)S(1)}, bf16[1024,384]{1,0:T(8,128)(2,1)S(1)}) custom-call(s32[1024,1]{1,0:T(8,128)S(1)} %copy-done.6, bf16[1024,384]{1,0:T(8,128)(2,1)S(1)} %copy-done.14, bf16[1024,384]{1,0:T(8,128)(2,1)S(1)} %copy-done.8, bf16[1024,384]{1,0:T(8,128)(2,1)S(1)} %copy-done.10, ...), custom_call_target="tpu_custom_call" | custom-call | flops 2415919104 | bytes 6291456 | tf_op jit(solution)/shard_map/attend_back/pallas_call | solution.py:140
  101.1 1.8 fusion.39
  102.9 1.7 fusion.44
  104.7 1.7 fusion.41
  106.8 3.3 %convolution_convert_fusion.5 = bf16[768,384]{1,0:T(8,128)(2,1)} fusion(bf16[1024,384]{1,0:T(8,128)(2,1)S(1)} %get-tuple-element.32, bf16[512,768]{1,0:T(8,128)(2,1)} %copy-done.42, bf16[512,768]{1,0:T(8,128)(2,1)} %copy-done.40), kind=kOutput, calls=%fused_computation.62 | convolution fusion | flops 607420416 | bytes 2949120 | tf_op jit(solution)/shard_map/dot_general | solution.py:46
  110.1 1.8 convolution_convert_fusion.8.refs_2_
  111.9 2.7 add_convert_fusion.1
  121.5 1.6 add_convert_fusion
  124.2 143.4 %sum_over_groups.1 = (bf16[1536,768]{1,0:T(8,128)(2,1)}, bf16[768,1536]{1,0:T(8,128)(2,1)}, bf16[768,384]{1,0:T(8,128)(2,1)S(1)}, bf16[768,384]{1,0:T(8,128)(2,1...) custom-call(bf16[1536,768]{1,0:T(8,128)(2,1)} %convolution_convert_fusion.1.refs_0_, ...), custom_call_target="tpu_custom_call" | custom-call | tf_op jit(solution)/shard_map/sum_over_groups/pallas_call | solution.py:280
  271.1 2.8 convert_element_type.190
  273.9 2.5 convert_element_type.191
  (240 shorter events, 45.8 us)
Async XLA Ops:
  0.7 38.8 %copy-start = (bf16[768,1536]{1,0:T(8,128)(2,1)S(1)}, bf16[768,1536]{1,0:T(8,128)(2,1)}, u32[]{:S(2)}) copy-start(bf16[768,1536]{1,0:T(8,128)(2,1)} %param.33) | copy-start | bytes 7077892
  0.7 4.8 %copy-start.64 = (bf16[384]{0:T(512)(128)(2,1)S(1)}, bf16[384]{0:T(512)(128)(2,1)}, u32[]{:S(2)}) copy-start(bf16[384]{0:T(512)(128)(2,1)} %param.28) | copy-start | bytes 2308
  0.7 4.8 %copy-start.65 = (bf16[384]{0:T(512)(128)(2,1)S(1)}, bf16[384]{0:T(512)(128)(2,1)}, u32[]{:S(2)}) copy-start(bf16[384]{0:T(512)(128)(2,1)} %param.27) | copy-start | bytes 2308
  0.7 4.8 %copy-start.63 = (s32[48]{0:T(128)S(1)}, s32[48]{0:T(128)}, u32[]{:S(2)}) copy-start(s32[48]{0:T(128)} %param.20) | copy-start | bytes 580
  0.7 4.8 %copy-start.55 = (s32[48]{0:T(128)S(1)}, s32[48]{0:T(128)}, u32[]{:S(2)}) copy-start(s32[48]{0:T(128)} %param.21) | copy-start | bytes 580
  5.0 3.2 %collective-permute-start = (bf16[512,768]{1,0:T(8,128)(2,1)}, bf16[512,768]{1,0:T(8,128)(2,1)}, u32[]{:S(2)}, u32[]{:S(2)}) collective-permute-start(bf16[512,768]{1,0:T(8,128)(2,1)} %fusion.14), channel_id=1, source_target_pairs={{0,1},{1,0},{2,3},{3,2},{4,5},{5,4},{6,7},{7,6},{8,9},{9,8},{10,11... | collective-permute-start | bytes 2359304 | tf_op jit(solution)/shard_map/ppermute | solution.py:157
  14.1 13.9 %copy-start.13 = (bf16[1024,384]{1,0:T(8,128)(2,1)}, bf16[1024,384]{1,0:T(8,128)(2,1)S(1)}, u32[]{:S(2)}) copy-start(bf16[1024,384]{1,0:T(8,128)(2,1)S(1)} %fusion.34.query_ref) | copy-start | bytes 2359300
  14.1 15.1 %copy-start.29 = (bf16[384,768]{1,0:T(8,128)(2,1)S(1)}, bf16[384,768]{1,0:T(8,128)(2,1)}, u32[]{:S(2)}) copy-start(bf16[384,768]{1,0:T(8,128)(2,1)} %param.29) | copy-start | bytes 1769476
  30.6 2.6 collective-permute-start.1
  37.1 6.0 %copy-start.44 = (bf16[512,768]{1,0:T(8,128)(2,1)}, bf16[512,768]{1,0:T(8,128)(2,1)S(1)}, u32[]{:S(2)}) copy-start(bf16[512,768]{1,0:T(8,128)(2,1)S(1)} %add_convert_fusion.3) | copy-start | bytes 2359300
  37.1 2.4 collective-permute-start.2
  37.5 5.6 %copy-start.36 = (bf16[512,768]{1,0:T(8,128)(2,1)}, bf16[512,768]{1,0:T(8,128)(2,1)S(1)}, u32[]{:S(2)}) copy-start(bf16[512,768]{1,0:T(8,128)(2,1)S(1)} %get-tuple-element.101) | copy-start | bytes 2359300
  37.6 5.6 %collective-permute-start.4 = (bf16[512,768]{1,0:T(8,128)(2,1)S(1)}, bf16[512,768]{1,0:T(8,128)(2,1)S(1)}, u32[]{:S(2)}, u32[]{:S(2)}) collective-permute-start(bf16[512,768]{1,0:T(8,128)(2,1)S(1)} %get-tuple-element.101), channel_id=1, source_target_pairs={{0,1},{1,0},{2,3},{3,2},{4,5},{5,4},{6,7},{7,6},{8,9},{9,8},{10,11... | collective-permute-start | bytes 2359304 | tf_op jit(solution)/shard_map/ppermute | solution.py:157
  38.0 5.2 %copy-start.66 = (bf16[1536,768]{1,0:T(8,128)(2,1)S(1)}, bf16[1536,768]{1,0:T(8,128)(2,1)}, u32[]{:S(2)}) copy-start(bf16[1536,768]{1,0:T(8,128)(2,1)} %param.35) | copy-start | bytes 7077892
  43.1 10.0 %copy-start.72 = (bf16[1024,1536]{1,0:T(8,128)(2,1)}, bf16[1024,1536]{1,0:T(8,128)(2,1)S(1)}, u32[]{:S(2)}) copy-start(bf16[1024,1536]{1,0:T(8,128)(2,1)S(1)} %get-tuple-element.125) | copy-start | bytes 9437188
  43.1 7.5 %copy-start.38 = (bf16[512,768]{1,0:T(8,128)(2,1)}, bf16[512,768]{1,0:T(8,128)(2,1)S(1)}, u32[]{:S(2)}) copy-start(bf16[512,768]{1,0:T(8,128)(2,1)S(1)} %collective-permute-done.4) | copy-start | bytes 2359300
  52.9 4.1 %collective-permute-start.5 = (bf16[512,768]{1,0:T(8,128)(2,1)}, bf16[512,768]{1,0:T(8,128)(2,1)}, u32[]{:S(2)}, u32[]{:S(2)}) collective-permute-start(bf16[512,768]{1,0:T(8,128)(2,1)} %fusion.31), channel_id=1, source_target_pairs={{0,1},{1,0},{2,3},{3,2},{4,5},{5,4},{6,7},{7,6},{8,9},{9,8},{10,11... | collective-permute-start | bytes 2359304 | tf_op jit(solution)/shard_map/ppermute | solution.py:157
  55.3 5.7 %collective-permute-start.3 = (bf16[512,768]{1,0:T(8,128)(2,1)}, bf16[512,768]{1,0:T(8,128)(2,1)}, u32[]{:S(2)}, u32[]{:S(2)}) collective-permute-start(bf16[512,768]{1,0:T(8,128)(2,1)} %fusion.28), channel_id=1, source_target_pairs={{0,1},{1,0},{2,3},{3,2},{4,5},{5,4},{6,7},{7,6},{8,9},{9,8},{10,11... | collective-permute-start | bytes 2359304 | tf_op jit(solution)/shard_map/ppermute | solution.py:157
  61.3 5.4 %copy-start.71 = (bf16[1024,1536]{1,0:T(8,128)(2,1)S(1)}, bf16[1024,1536]{1,0:T(8,128)(2,1)}, u32[]{:S(2)}) copy-start(bf16[1024,1536]{1,0:T(8,128)(2,1)} %copy-done.70) | copy-start | bytes 9437188
  66.5 10.6 %collective-permute-start.6 = (bf16[512,768]{1,0:T(8,128)(2,1)S(1)}, bf16[512,768]{1,0:T(8,128)(2,1)}, u32[]{:S(2)}, u32[]{:S(2)}) collective-permute-start(bf16[512,768]{1,0:T(8,128)(2,1)S(1)} %multiply_convert_fusion.1), channel_id=1, source_target_pairs={{0,1},{1,0},{2,3},{3,2},{4,5},{5,4},{6,7},{7,6},{8,9},{9,8},{10,11... | collective-permute-start | bytes 2359304 | tf_op jit(solution)/shard_map/ppermute | solution.py:157
  81.6 19.5 %copy-start.32 = (bf16[768,384]{1,0:T(8,128)(2,1)S(1)}, bf16[768,384]{1,0:T(8,128)(2,1)}, u32[]{:S(2)}) copy-start(bf16[768,384]{1,0:T(8,128)(2,1)} %param.25) | copy-start | bytes 1769476
  114.7 3.4 %collective-permute-start.7 = (bf16[512,768]{1,0:T(8,128)(2,1)S(1)}, bf16[512,768]{1,0:T(8,128)(2,1)S(1)}, u32[]{:S(2)}, u32[]{:S(2)}) collective-permute-start(bf16[512,768]{1,0:T(8,128)(2,1)S(1)} %add_convert_fusion.1), channel_id=1, source_target_pairs={{0,1},{1,0},{2,3},{3,2},{4,5},{5,4},{6,7},{7,6},{8,9},{9,8},{10,11... | collective-permute-start | bytes 2359304 | tf_op jit(solution)/shard_map/ppermute | solution.py:157
  120.8 2.3 collective-permute-start.8
  279.3 6.4 %copy-start.1 = (bf16[768,1536]{1,0:T(8,128)(2,1)S(1)}, bf16[768,1536]{1,0:T(8,128)(2,1)}, u32[]{:S(2)}) copy-start(bf16[768,1536]{1,0:T(8,128)(2,1)} %param.33) | copy-start | bytes 7077892
  (59 other events, 129.0 us)

commit v2 on v1

--- a/solution.py
+++ b/solution.py
@@ -272,6 +272,7 @@
         else:
             cuts = [(0, width, index - 3)]
         chains += [(index,) + cut for cut in cuts]
+    chains.sort(key=lambda chain: (chain[0] > 1, chain[3] != 2))
     count = len(arrays)
     slots = len(chains) * 2 * len(bits)
     shapes = [jax.ShapeDtypeStruct(array.shape, array.dtype) for array in arrays]

time: 290 us -> 289 us (level)
  no operation moved by 1% of the time
where the time goes in v2:
time: 289 us; the launch traced here: 284 us
  Pallas kernels  175 us (61%)
  matrix products  58 us (20%)
  other arithmetic  23.7 us (8%)
  local copies, waits for them, and re-layouts  19.7 us (7%)
  waiting for transfers between devices  3.89 us (1%)
    pallas_call x1, Pallas kernels, sum_over_groups(): pl.pallas_call(functools.partial(sum_kernel, groups, orders, chains, coun...  142 us
    pallas_call x2, Pallas kernels, attention_call(): pl.pallas_call(kernel, grid=(width // (2 * HD),), in_specs=[pl.BlockSpec(...  33.4 us
    dot_general x10, matrix products, transposed_product(): lax.dot_general(left, right, (((1,), (1,)), ((), ())), preferred_element_...  24.4 us
    dot_general x6, matrix products, rows_product(): lax.dot_general(left, right, (((0,), (0,)), ((), ())), preferred_element_...  17 us
    unnamed x149, local copies, waits for them, and re-layouts  11.2 us
    dot_general x2, matrix products, on_device(): jnp.dot(rows, contract_weight, preferred_element_type=jnp.float32)  6.29 us
    slice x10, local copies, waits for them, and re-layouts, on_device(): cuts.append(small[at:at + size])  6.18 us
  transfers between devices with their start and end apart: 9, of which 2 were waited for; matrix products, arithmetic and copies ran while one was open for 10% of the time, Pallas kernels for 0%

profile of v2, /device:TPU:0, one launch (start us, length us, event | category | flops | bytes accessed | tf_op | source)
XLA Modules:
  0.0 284.2 jit_solution(5350199883629985228)
XLA Ops:
  8.2 1.7 broadcast_select_fusion.3
  14.1 13.9 %attend.1 = (bf16[1024,384]{1,0:T(8,128)(2,1)S(1)}, f32[1024,384]{1,0:T(8,128)S(1)}) custom-call(s32[1024,1]{1,0:T(8,128)S(1)} %copy-done.5, bf16[1024,384]{1,0:T(8,128)(2,1)S(1)} %fusion.34.query_ref, bf16[1024,384]{1,0:T(8,128)(2,1)S(1)} %convolution_convert_fusion.3.keys_ref, bf16[1024,384]{1,0:T(8,128)(2,1)S(1)} %add_convert_fusion.4.values_ref), custom_call_target="tpu_custom_call" | custom-call | flops 1207959552 | bytes 6291456 | tf_op jit(solution)/shard_map/attend/pallas_call | solution.py:140
  30.8 2.4 collective-permute-done.1
  33.3 2.3 fusion.81
  39.4 3.7 %multiply_convert_fusion = (bf16[1024,1536]{1,0:T(8,128)(2,1)S(1)}, f32[1024,1536]{1,0:T(8,128)S(1)}) fusion(f32[1536]{0:T(1024)S(1)} %convert_element_type.161, bf16[768,1536]{1,0:T(8,128)(2,1)S(1)} %copy-done, bf16[512,768]{1,0:T(8,128)(2,1)S(1)} %collective-permute-done.2, bf16[512,768]{1,0:T(8,128)(2,1)S(1)} %add_convert_fusion.3), kind=kOutput, calls=%fused_computation.9 | convolution fusion | flops 2434793472 | bytes 13375488 | tf_op jit(solution)/shard_map/dot_general | solution.py:379
  43.2 7.4 %fusion.82 = (bf16[1536]{0:T(1024)(128)(2,1)S(1)}, bf16[1024,1536]{1,0:T(8,128)(2,1)S(1)}) fusion(f32[1024,1536]{1,0:T(8,128)S(1)} %get-tuple-element.126, f32[1536]{0:T(1024)S(1)} %convert_element_type.161, bf16[1536,768]{1,0:T(8,128)(2,1)S(1)} %copy-done.66, bf16[512,768]{1,0:T(8,128)(2,1)S(1)} %collective-permute-done.4, ...), kind=kOutput, calls=%fused_computation.139 | convolution fusion | flops 2453666304 | bytes 13378560 | tf_op jit(solution)/shard_map/dot_general | solution.py:52
  50.6 2.3 fusion.31
  53.1 2.3 fusion.28
  57.1 4.0 %multiply_reduce_fusion = (f32[768]{0:T(1024)S(1)}, f32[512]{0:T(512)S(1)}, f32[768]{0:T(1024)S(1)}, f32[512,768]{1,0:T(8,128)S(1)}) fusion(f32[512,768]{1,0:T(8,128)} %copy-done.17, f32[512]{0:T(512)S(1)} %fusion.67, f32[512]{0:T(512)S(1)} %broadcast_multiply_fusion, bf16[512,768]{1,0:T(8,128)(2,1)} %collective-permute-done.5, ...), kind=kOutput, calls=%fused_computation.44 | convolution fusion | flops 1211889664 | bytes 7879680 | tf_op jit(solution)/shard_map/dot_general | solution.py:52
  61.3 4.0 %fusion.79 = (f32[512]{0:T(512)S(1)}, f32[512,768]{1,0:T(8,128)S(1)}, bf16[512,768]{1,0:T(8,128)(2,1)}) fusion(f32[512]{0:T(512)S(1)} %multiply_multiply_fusion.3, f32[512,768]{1,0:T(8,128)S(1)} %copy-done.18, f32[512]{0:T(512)S(1)} %broadcast_multiply_fusion, f32[512]{0:T(512)S(1)} %fusion.67, f32[768]{0:T(1024)S(1)} %convert_element_type.158, ...), kind=kOutput, calls=%fused_computation.136 | convolution fusion | flops 1213857280 | bytes 11028480 | tf_op jit(solution)/shard_map/dot_general | solution.py:394
  67.3 3.9 %convolution_convert_fusion.refs_1_ = bf16[768,1536]{1,0:T(8,128)(2,1)} fusion(bf16[1024,1536]{1,0:T(8,128)(2,1)S(1)} %copy-done.71, bf16[512,768]{1,0:T(8,128)(2,1)S(1)} %copy-done.69, bf16[512,768]{1,0:T(8,128)(2,1)S(1)} %copy-done.45), kind=kOutput, calls=%fused_computation.10 | convolution fusion | flops 2420244480 | bytes 7077888 | tf_op jit(solution)/shard_map/dot_general | solution.py:46
  71.2 6.0 %convolution_convert_fusion.1.refs_0_ = bf16[1536,768]{1,0:T(8,128)(2,1)} fusion(bf16[1024,1536]{1,0:T(8,128)(2,1)} %copy-done.72, bf16[512,768]{1,0:T(8,128)(2,1)S(1)} %copy-done.39, bf16[512,768]{1,0:T(8,128)(2,1)S(1)} %copy-done.37), kind=kOutput, calls=%fused_computation.11 | convolution fusion | flops 2420244480 | bytes 7077888 | tf_op jit(solution)/shard_map/dot_general | solution.py:46
  77.2 1.6 fusion.78
  81.6 19.5 %attend_back.1 = (bf16[1024,384]{1,0:T(8,128)(2,1)S(1)}, bf16[1024,384]{1,0:T(8,128)(2,1)S(1)}, bf16[1024,384]{1,0:T(8,128)(2,1)S(1)}) custom-call(s32[1024,1]{1,0:T(8,128)S(1)} %copy-done.6, bf16[1024,384]{1,0:T(8,128)(2,1)S(1)} %copy-done.14, bf16[1024,384]{1,0:T(8,128)(2,1)S(1)} %copy-done.8, bf16[1024,384]{1,0:T(8,128)(2,1)S(1)} %copy-done.10, ...), custom_call_target="tpu_custom_call" | custom-call | flops 2415919104 | bytes 6291456 | tf_op jit(solution)/shard_map/attend_back/pallas_call | solution.py:140
  101.1 1.8 fusion.39
  102.9 1.7 fusion.44
  104.7 1.7 fusion.41
  106.8 3.3 %convolution_convert_fusion.5 = bf16[768,384]{1,0:T(8,128)(2,1)} fusion(bf16[1024,384]{1,0:T(8,128)(2,1)S(1)} %get-tuple-element.32, bf16[512,768]{1,0:T(8,128)(2,1)} %copy-done.42, bf16[512,768]{1,0:T(8,128)(2,1)} %copy-done.40), kind=kOutput, calls=%fused_computation.62 | convolution fusion | flops 607420416 | bytes 2949120 | tf_op jit(solution)/shard_map/dot_general | solution.py:46
  110.1 1.8 convolution_convert_fusion.8.refs_2_
  111.9 2.7 add_convert_fusion.1
  121.5 1.6 add_convert_fusion
  124.2 141.7 %sum_over_groups.1 = (bf16[1536,768]{1,0:T(8,128)(2,1)}, bf16[768,1536]{1,0:T(8,128)(2,1)}, bf16[768,384]{1,0:T(8,128)(2,1)S(1)}, bf16[768,384]{1,0:T(8,128)(2,1...) custom-call(bf16[1536,768]{1,0:T(8,128)(2,1)} %convolution_convert_fusion.1.refs_0_, ...), custom_call_target="tpu_custom_call" | custom-call | tf_op jit(solution)/shard_map/sum_over_groups/pallas_call | solution.py:281
  269.4 2.8 convert_element_type.190
  272.2 2.5 convert_element_type.191
  (240 shorter events, 45.8 us)
Async XLA Ops:
  0.7 38.8 %copy-start = (bf16[768,1536]{1,0:T(8,128)(2,1)S(1)}, bf16[768,1536]{1,0:T(8,128)(2,1)}, u32[]{:S(2)}) copy-start(bf16[768,1536]{1,0:T(8,128)(2,1)} %param.33) | copy-start | bytes 7077892
  0.7 4.8 %copy-start.64 = (bf16[384]{0:T(512)(128)(2,1)S(1)}, bf16[384]{0:T(512)(128)(2,1)}, u32[]{:S(2)}) copy-start(bf16[384]{0:T(512)(128)(2,1)} %param.28) | copy-start | bytes 2308
  0.7 4.8 %copy-start.65 = (bf16[384]{0:T(512)(128)(2,1)S(1)}, bf16[384]{0:T(512)(128)(2,1)}, u32[]{:S(2)}) copy-start(bf16[384]{0:T(512)(128)(2,1)} %param.27) | copy-start | bytes 2308
  0.7 4.8 %copy-start.63 = (s32[48]{0:T(128)S(1)}, s32[48]{0:T(128)}, u32[]{:S(2)}) copy-start(s32[48]{0:T(128)} %param.20) | copy-start | bytes 580
  0.7 4.8 %copy-start.55 = (s32[48]{0:T(128)S(1)}, s32[48]{0:T(128)}, u32[]{:S(2)}) copy-start(s32[48]{0:T(128)} %param.21) | copy-start | bytes 580
  5.0 3.2 %collective-permute-start = (bf16[512,768]{1,0:T(8,128)(2,1)}, bf16[512,768]{1,0:T(8,128)(2,1)}, u32[]{:S(2)}, u32[]{:S(2)}) collective-permute-start(bf16[512,768]{1,0:T(8,128)(2,1)} %fusion.14), channel_id=1, source_target_pairs={{0,1},{1,0},{2,3},{3,2},{4,5},{5,4},{6,7},{7,6},{8,9},{9,8},{10,11... | collective-permute-start | bytes 2359304 | tf_op jit(solution)/shard_map/ppermute | solution.py:157
  14.1 13.9 %copy-start.13 = (bf16[1024,384]{1,0:T(8,128)(2,1)}, bf16[1024,384]{1,0:T(8,128)(2,1)S(1)}, u32[]{:S(2)}) copy-start(bf16[1024,384]{1,0:T(8,128)(2,1)S(1)} %fusion.34.query_ref) | copy-start | bytes 2359300
  14.1 15.1 %copy-start.29 = (bf16[384,768]{1,0:T(8,128)(2,1)S(1)}, bf16[384,768]{1,0:T(8,128)(2,1)}, u32[]{:S(2)}) copy-start(bf16[384,768]{1,0:T(8,128)(2,1)} %param.29) | copy-start | bytes 1769476
  30.6 2.6 collective-permute-start.1
  37.1 6.0 %copy-start.44 = (bf16[512,768]{1,0:T(8,128)(2,1)}, bf16[512,768]{1,0:T(8,128)(2,1)S(1)}, u32[]{:S(2)}) copy-start(bf16[512,768]{1,0:T(8,128)(2,1)S(1)} %add_convert_fusion.3) | copy-start | bytes 2359300
  37.1 2.4 collective-permute-start.2
  37.5 5.6 %copy-start.36 = (bf16[512,768]{1,0:T(8,128)(2,1)}, bf16[512,768]{1,0:T(8,128)(2,1)S(1)}, u32[]{:S(2)}) copy-start(bf16[512,768]{1,0:T(8,128)(2,1)S(1)} %get-tuple-element.101) | copy-start | bytes 2359300
  37.6 5.6 %collective-permute-start.4 = (bf16[512,768]{1,0:T(8,128)(2,1)S(1)}, bf16[512,768]{1,0:T(8,128)(2,1)S(1)}, u32[]{:S(2)}, u32[]{:S(2)}) collective-permute-start(bf16[512,768]{1,0:T(8,128)(2,1)S(1)} %get-tuple-element.101), channel_id=1, source_target_pairs={{0,1},{1,0},{2,3},{3,2},{4,5},{5,4},{6,7},{7,6},{8,9},{9,8},{10,11... | collective-permute-start | bytes 2359304 | tf_op jit(solution)/shard_map/ppermute | solution.py:157
  38.0 5.2 %copy-start.66 = (bf16[1536,768]{1,0:T(8,128)(2,1)S(1)}, bf16[1536,768]{1,0:T(8,128)(2,1)}, u32[]{:S(2)}) copy-start(bf16[1536,768]{1,0:T(8,128)(2,1)} %param.35) | copy-start | bytes 7077892
  43.1 10.0 %copy-start.72 = (bf16[1024,1536]{1,0:T(8,128)(2,1)}, bf16[1024,1536]{1,0:T(8,128)(2,1)S(1)}, u32[]{:S(2)}) copy-start(bf16[1024,1536]{1,0:T(8,128)(2,1)S(1)} %get-tuple-element.125) | copy-start | bytes 9437188
  43.1 7.5 %copy-start.38 = (bf16[512,768]{1,0:T(8,128)(2,1)}, bf16[512,768]{1,0:T(8,128)(2,1)S(1)}, u32[]{:S(2)}) copy-start(bf16[512,768]{1,0:T(8,128)(2,1)S(1)} %collective-permute-done.4) | copy-start | bytes 2359300
  52.9 4.1 %collective-permute-start.5 = (bf16[512,768]{1,0:T(8,128)(2,1)}, bf16[512,768]{1,0:T(8,128)(2,1)}, u32[]{:S(2)}, u32[]{:S(2)}) collective-permute-start(bf16[512,768]{1,0:T(8,128)(2,1)} %fusion.31), channel_id=1, source_target_pairs={{0,1},{1,0},{2,3},{3,2},{4,5},{5,4},{6,7},{7,6},{8,9},{9,8},{10,11... | collective-permute-start | bytes 2359304 | tf_op jit(solution)/shard_map/ppermute | solution.py:157
  55.3 5.7 %collective-permute-start.3 = (bf16[512,768]{1,0:T(8,128)(2,1)}, bf16[512,768]{1,0:T(8,128)(2,1)}, u32[]{:S(2)}, u32[]{:S(2)}) collective-permute-start(bf16[512,768]{1,0:T(8,128)(2,1)} %fusion.28), channel_id=1, source_target_pairs={{0,1},{1,0},{2,3},{3,2},{4,5},{5,4},{6,7},{7,6},{8,9},{9,8},{10,11... | collective-permute-start | bytes 2359304 | tf_op jit(solution)/shard_map/ppermute | solution.py:157
  61.3 5.4 %copy-start.71 = (bf16[1024,1536]{1,0:T(8,128)(2,1)S(1)}, bf16[1024,1536]{1,0:T(8,128)(2,1)}, u32[]{:S(2)}) copy-start(bf16[1024,1536]{1,0:T(8,128)(2,1)} %copy-done.70) | copy-start | bytes 9437188
  66.5 10.6 %collective-permute-start.6 = (bf16[512,768]{1,0:T(8,128)(2,1)S(1)}, bf16[512,768]{1,0:T(8,128)(2,1)}, u32[]{:S(2)}, u32[]{:S(2)}) collective-permute-start(bf16[512,768]{1,0:T(8,128)(2,1)S(1)} %multiply_convert_fusion.1), channel_id=1, source_target_pairs={{0,1},{1,0},{2,3},{3,2},{4,5},{5,4},{6,7},{7,6},{8,9},{9,8},{10,11... | collective-permute-start | bytes 2359304 | tf_op jit(solution)/shard_map/ppermute | solution.py:157
  81.6 19.5 %copy-start.32 = (bf16[768,384]{1,0:T(8,128)(2,1)S(1)}, bf16[768,384]{1,0:T(8,128)(2,1)}, u32[]{:S(2)}) copy-start(bf16[768,384]{1,0:T(8,128)(2,1)} %param.25) | copy-start | bytes 1769476
  114.7 3.4 %collective-permute-start.7 = (bf16[512,768]{1,0:T(8,128)(2,1)S(1)}, bf16[512,768]{1,0:T(8,128)(2,1)S(1)}, u32[]{:S(2)}, u32[]{:S(2)}) collective-permute-start(bf16[512,768]{1,0:T(8,128)(2,1)S(1)} %add_convert_fusion.1), channel_id=1, source_target_pairs={{0,1},{1,0},{2,3},{3,2},{4,5},{5,4},{6,7},{7,6},{8,9},{9,8},{10,11... | collective-permute-start | bytes 2359304 | tf_op jit(solution)/shard_map/ppermute | solution.py:157
  120.8 2.3 collective-permute-start.8
  277.6 6.4 %copy-start.1 = (bf16[768,1536]{1,0:T(8,128)(2,1)S(1)}, bf16[768,1536]{1,0:T(8,128)(2,1)}, u32[]{:S(2)}) copy-start(bf16[768,1536]{1,0:T(8,128)(2,1)} %param.33) | copy-start | bytes 7077892
  (59 other events, 129.0 us)
